TPU v7x, 32 devices: a whole 2x2x4 slice. The times are simulated.
32 devices in a mesh: nodes: 8 (over z, y), cols: 4 (over x, core).
Axes of the slice: x: 2, y: 2, z: 4, core: 2. Of those that a mesh axis runs over, the one named last changes fastest.
Arguments:
- vectors: bfloat16 [32, 4, 6, 16, 512], P('nodes', None, None, None, 'cols'), may hold values from -6 to 6
- node_shift: bfloat16 [32, 6, 16], P('nodes'), may hold values from 0.5 to 2
- coupling: float32 [4, 4], replicated, may hold values from -3 to 3
- dual_basis: bfloat16 [12288, 512], P(('nodes', 'cols')), may hold values from -0.0546875 to 0.0546875
Outputs:
- gram_matrix: float32 [512, 512], P('cols')
- rotated: bfloat16 [12288, 512], P(('nodes', 'cols'))
All inputs are finite; a program needn't handle non-finite values.
Results may differ from a plain program's by a relative error of at most 0.0064.
Values may be sent and summed in bfloat16 or wider, within the bound.
A program may use at most 64 MiB of HBM per device.

v0:
```python
import jax
import jax.numpy as jnp
from jax import lax
from jax.sharding import PartitionSpec as P

center_value = 10.0
half_width = 7.0


def with_halo(block, sides, width):
    for axis, dim in sides:
        count = lax.axis_size(axis)
        forward = [(i, i + 1) for i in range(count - 1)]
        backward = [(target, source) for source, target in forward]
        low = lax.ppermute(
            lax.slice_in_dim(block, block.shape[dim] - width, None, axis=dim), axis, forward
        )
        high = lax.ppermute(lax.slice_in_dim(block, 0, width, axis=dim), axis, backward)
        block = jnp.concatenate([low, block, high], axis=dim)
    return block


def operate_inner(padded, shift_part, coupling):
    middle = padded[1:-1]
    beside = padded[2:] + padded[:-2]
    spread = jnp.pad(middle, ((0, 0), (0, 0), (1, 1), (1, 1), (0, 0)))
    beside = beside + spread[:, :, 2:, 1:-1] + spread[:, :, :-2, 1:-1]
    beside = beside + spread[:, :, 1:-1, 2:] + spread[:, :, 1:-1, :-2]
    coupled = jnp.einsum("de,xeyzc->xdyzc", coupling, middle, precision=lax.Precision.HIGHEST)
    return (6.0 + shift_part[:, None, :, :, None]) * middle - beside + coupled


def shards(vectors, node_shift, coupling, dual_basis):
    shift_full = node_shift.astype(jnp.float32)

    def advance(state):
        padded = with_halo(state, (("nodes", 0),), 1)
        return operate_inner(padded, shift_full, coupling) - center_value * state

    state_zero = vectors.astype(jnp.float32)
    state_one = advance(state_zero) / half_width
    state_two = 2.0 * advance(state_one) / half_width - state_zero
    state_three = 2.0 * advance(state_two) / half_width - state_one
    filtered = state_three.astype(jnp.bfloat16).reshape(-1, state_three.shape[-1])
    row_stack = lax.all_to_all(filtered, "cols", split_axis=0, concat_axis=1, tiled=True)
    partial_gram = lax.dot_general(
        dual_basis, row_stack, (((0,), (0,)), ((), ())), preferred_element_type=jnp.float32
    )
    vector_count = dual_basis.shape[1]
    own_rows = lax.psum_scatter(partial_gram, "cols", scatter_dimension=0, tiled=True)
    own_rows = lax.psum(own_rows, "nodes")
    rotated_sum = jnp.dot(
        row_stack,
        lax.all_gather(own_rows.astype(jnp.bfloat16), "cols", axis=0, tiled=True),
        preferred_element_type=jnp.float32,
    )
    rotated = (rotated_sum * vector_count ** (-0.5)).astype(jnp.bfloat16)
    return (own_rows, rotated)


def solution(mesh):
    placed = (
        P("nodes", None, None, None, "cols"),
        P("nodes", None, None),
        P(),
        P(("nodes", "cols"), None),
    )
    return jax.shard_map(
        shards,
        mesh=mesh,
        in_specs=placed,
        out_specs=(P("cols", None), P(("nodes", "cols"), None)),
        check_vma=False,
    )
```

profile of v0, /device:TPU:27, one launch (start us, length us, event | category | flops | bytes accessed | tf_op | source)
XLA Modules:
  0.0 184.1 jit_solution(7897869612966135732)
XLA Ops:
  7.2 0.0 copy-start
  7.2 0.0 reduce-scatter.2.cloned.1.call-start
  7.3 1.3 copy_convert_fusion
  8.6 3.0 %collective-permute-start = (f32[1,4,6,16,128]{4,1,3,2,0:T(4,128)S(1)}, f32[1,4,6,16,128]{4,1,3,2,0:T(4,128)S(1)}, u32[]{:S(2)}, u32[]{:S(2)}) collective-permute-start(f32[1,4,6,16,128]{4,1,3,2,0:T(4,128)S(1)} %get-tuple-element.10), channel_id=1, source_target_pairs={{4,0},{8,4},{12,8},{16,12},{20,16},{24,20},{28,24},{5,1},{9,5},{13... | collective-permute-start | bytes 589832 | tf_op jit(solution)/shard_map/ppermute | solution.py:18
  11.6 2.3 %collective-permute-start.1 = (f32[1,4,6,16,128]{4,1,3,2,0:T(4,128)S(1)}, f32[1,4,6,16,128]{4,1,3,2,0:T(4,128)S(1)}, u32[]{:S(2)}, u32[]{:S(2)}) collective-permute-start(f32[1,4,6,16,128]{4,1,3,2,0:T(4,128)S(1)} %get-tuple-element.11), channel_id=1, source_target_pairs={{0,4},{4,8},{8,12},{12,16},{16,20},{20,24},{24,28},{1,5},{5,9},{9,... | collective-permute-start | bytes 589832 | tf_op jit(solution)/shard_map/ppermute | solution.py:15
  13.9 0.0 copy-done.3
  13.9 2.3 %collective-permute-done = f32[1,4,6,16,128]{4,1,3,2,0:T(4,128)S(1)} collective-permute-done((f32[1,4,6,16,128]{4,1,3,2,0:T(4,128)S(1)}, f32[1,4,6,16,128]{4,1,3,2,0:T(4,128)S(1)}, u32[]{:S(2)}, u32[]{:S(2)}) %collective-permute-start) | collective-permute-done | bytes 196640 | tf_op jit(solution)/shard_map/ppermute | solution.py:18
  16.2 3.7 %collective-permute-done.1 = f32[1,4,6,16,128]{4,1,3,2,0:T(4,128)S(1)} collective-permute-done((f32[1,4,6,16,128]{4,1,3,2,0:T(4,128)S(1)}, f32[1,4,6,16,128]{4,1,3,2,0:T(4,128)S(1)}, u32[]{:S(2)}, u32[]{:S(2)}) %collective-permute-start.1) | collective-permute-done | bytes 196640 | tf_op jit(solution)/shard_map/ppermute | solution.py:15
  19.9 2.2 %broadcast_multiply_fusion = (f32[4,4,6,16,128]{4,1,3,2,0:T(4,128)S(1)}, f32[4,4,6,16,128]{4,1,3,2,0:T(4,128)S(1)}) fusion(f32[4,4,6,16,128]{4,1,3,2,0:T(4,128)S(1)} %copy_convert_fusion, f32[4,4]{1,0:T(4,128)S(1)} %copy-done.4, bf16[4,4,6,16,128]{4,3,2,1,0:T(8,128)(2,1)S(1)} %copy-done.2, f32[1,4,6,16,128]{4,1,3,2,0:T(4,128)S(1)} %collective-permute-done.1, ...), kind=kOutput, calls=%fused_computation.53 | convolution fusion | flops 11993088 | bytes 3147328 | tf_op jit(solution)/shard_map/de,xeyzc->xdyzc/dot_general | solution.py:29
  22.2 5.5 %collective-permute-start.2 = (f32[1,4,6,16,128]{4,1,3,2,0:T(4,128)S(1)}, f32[1,4,6,16,128]{4,1,3,2,0:T(4,128)S(1)}, u32[]{:S(2)}, u32[]{:S(2)}) collective-permute-start(f32[1,4,6,16,128]{4,1,3,2,0:T(4,128)S(1)} %get-tuple-element.8), channel_id=1, source_target_pairs={{4,0},{8,4},{12,8},{16,12},{20,16},{24,20},{28,24},{5,1},{9,5},{13... | collective-permute-start | bytes 589832 | tf_op jit(solution)/shard_map/ppermute | solution.py:18
  27.7 1.9 %collective-permute-start.3 = (f32[1,4,6,16,128]{4,1,3,2,0:T(4,128)S(1)}, f32[1,4,6,16,128]{4,1,3,2,0:T(4,128)S(1)}, u32[]{:S(2)}, u32[]{:S(2)}) collective-permute-start(f32[1,4,6,16,128]{4,1,3,2,0:T(4,128)S(1)} %get-tuple-element.9), channel_id=1, source_target_pairs={{0,4},{4,8},{8,12},{12,16},{16,20},{20,24},{24,28},{1,5},{5,9},{9,... | collective-permute-start | bytes 589832 | tf_op jit(solution)/shard_map/ppermute | solution.py:15
  29.6 1.9 %collective-permute-done.2 = f32[1,4,6,16,128]{4,1,3,2,0:T(4,128)S(1)} collective-permute-done((f32[1,4,6,16,128]{4,1,3,2,0:T(4,128)S(1)}, f32[1,4,6,16,128]{4,1,3,2,0:T(4,128)S(1)}, u32[]{:S(2)}, u32[]{:S(2)}) %collective-permute-start.2) | collective-permute-done | bytes 196640 | tf_op jit(solution)/shard_map/ppermute | solution.py:18
  31.5 4.6 %collective-permute-done.3 = f32[1,4,6,16,128]{4,1,3,2,0:T(4,128)S(1)} collective-permute-done((f32[1,4,6,16,128]{4,1,3,2,0:T(4,128)S(1)}, f32[1,4,6,16,128]{4,1,3,2,0:T(4,128)S(1)}, u32[]{:S(2)}, u32[]{:S(2)}) %collective-permute-start.3) | collective-permute-done | bytes 196640 | tf_op jit(solution)/shard_map/ppermute | solution.py:15
  36.1 2.9 %fusion.3 = f32[4,4,6,16,128]{4,1,3,2,0:T(4,128)S(1)} fusion(f32[4,4,6,16,128]{4,1,3,2,0:T(4,128)S(1)} %get-tuple-element.14, f32[1,4,6,16,128]{4,1,3,2,0:T(4,128)S(1)} %collective-permute-done.3, f32[1,4,6,16,128]{4,1,3,2,0:T(4,128)S(1)} %collective-permute-done.2, f32[4,4,6,16,128]{4,1,3,2,0:T(4,128)S(1)} %get-tuple-element.15, ...), kind=kOutput, calls=%fused_computation.20 | convolution fusion | flops 12386304 | bytes 3950592 | tf_op jit(solution)/shard_map/de,xeyzc->xdyzc/dot_general | solution.py:29
  39.0 5.4 %collective-permute-start.4 = (f32[1,4,6,16,128]{4,1,3,2,0:T(4,128)S(1)}, f32[1,4,6,16,128]{4,1,3,2,0:T(4,128)S(1)}, u32[]{:S(2)}, u32[]{:S(2)}) collective-permute-start(f32[1,4,6,16,128]{4,1,3,2,0:T(4,128)S(1)} %get-tuple-element.6), channel_id=1, source_target_pairs={{4,0},{8,4},{12,8},{16,12},{20,16},{24,20},{28,24},{5,1},{9,5},{13... | collective-permute-start | bytes 589832 | tf_op jit(solution)/shard_map/ppermute | solution.py:18
  44.4 1.9 %collective-permute-start.5 = (f32[1,4,6,16,128]{4,1,3,2,0:T(4,128)S(1)}, f32[1,4,6,16,128]{4,1,3,2,0:T(4,128)S(1)}, u32[]{:S(2)}, u32[]{:S(2)}) collective-permute-start(f32[1,4,6,16,128]{4,1,3,2,0:T(4,128)S(1)} %get-tuple-element.7), channel_id=1, source_target_pairs={{0,4},{4,8},{8,12},{12,16},{16,20},{20,24},{24,28},{1,5},{5,9},{9,... | collective-permute-start | bytes 589832 | tf_op jit(solution)/shard_map/ppermute | solution.py:15
  46.3 1.9 %collective-permute-done.4 = f32[1,4,6,16,128]{4,1,3,2,0:T(4,128)S(1)} collective-permute-done((f32[1,4,6,16,128]{4,1,3,2,0:T(4,128)S(1)}, f32[1,4,6,16,128]{4,1,3,2,0:T(4,128)S(1)}, u32[]{:S(2)}, u32[]{:S(2)}) %collective-permute-start.4) | collective-permute-done | bytes 196640 | tf_op jit(solution)/shard_map/ppermute | solution.py:18
  48.2 4.7 %collective-permute-done.5 = f32[1,4,6,16,128]{4,1,3,2,0:T(4,128)S(1)} collective-permute-done((f32[1,4,6,16,128]{4,1,3,2,0:T(4,128)S(1)}, f32[1,4,6,16,128]{4,1,3,2,0:T(4,128)S(1)}, u32[]{:S(2)}, u32[]{:S(2)}) %collective-permute-start.5) | collective-permute-done | bytes 196640 | tf_op jit(solution)/shard_map/ppermute | solution.py:15
  52.9 2.9 %fusion.11 = bf16[4,4,6,16,128]{4,1,3,2,0:T(4,128)(2,1)S(1)} fusion(f32[4,4,6,16,128]{4,1,3,2,0:T(4,128)S(1)} %fusion.3, f32[1,4,6,16,128]{4,1,3,2,0:T(4,128)S(1)} %collective-permute-done.5, f32[1,4,6,16,128]{4,1,3,2,0:T(4,128)S(1)} %collective-permute-done.4, f32[4,6,16]{2,1,0:T(8,128)S(1)} %copy.11, f32[4,4]{1,0:T(4,128)S(1)} %copy-done.4, ...), kind=kOutput, calls=%fused_computation.28 | convolution fusion | flops 12582912 | bytes 3164160 | tf_op jit(solution)/shard_map/de,xeyzc->xdyzc/dot_general | solution.py:29
  55.8 0.1 copy.15
  55.9 9.9 %all_to_all.19 = bf16[4,384,128]{2,1,0:T(8,128)(2,1)S(1)} all-to-all(bf16[4,384,128]{2,1,0:T(8,128)(2,1)S(1)} %bitcast.52), channel_id=1, replica_groups=mesh['nodes'=8,'cols'=4] {'cols'}, dimensions={0} | all-to-all | bytes 786432 | tf_op jit(solution)/shard_map/all_to_all | solution.py:45
  65.8 0.2 copy.16
  66.0 1.4 convolution_bitcast_fusion
  67.4 0.0 reduce-scatter.2.cloned.1.call-update
  67.5 0.0 all-reduce.5.cloned.1.call-start
  67.5 25.3 %reduce-scatter.2.cloned.1.call-done = f32[128,512]{0,1:T(8,128)} async-done(((f32[512,512]{0,1:T(8,128)}), f32[128,512]{0,1:T(8,128)}) %reduce-scatter.2.cloned.1.call-update) | async-done | bytes 262160 | tf_op jit(solution)/shard_map/reduce_scatter | solution.py:50
  92.8 0.0 all-reduce.5.cloned.1.call-update
  92.8 72.4 %all-reduce.5.cloned.1.call-done = f32[128,512]{0,1:T(8,128)} async-done(((f32[128,512]{0,1:T(8,128)}), f32[128,512]{0,1:T(8,128)}) %all-reduce.5.cloned.1.call-update) | async-done | bytes 262160 | tf_op jit(solution)/shard_map/psum | solution.py:51
  165.3 1.0 convert_element_type.22
  166.2 9.0 %all_gather.3 = bf16[512,512]{0,1:T(8,128)(2,1)S(1)} all-gather(bf16[128,512]{0,1:T(8,128)(2,1)S(1)} %convert_element_type.22), channel_id=1, replica_groups=mesh['nodes'=8,'cols'=4] {'cols'}, dimensions={0}, use_global_device_ids=true | all-gather | bytes 655360 | tf_op jit(solution)/shard_map/all_gather | solution.py:54
  175.3 1.2 fusion.10
  176.4 0.8 copy.17
  (14 shorter events, 0.1 us)
Async XLA Ops:
  7.2 58.9 %copy-start = (bf16[384,512]{1,0:T(8,128)(2,1)S(1)}, bf16[384,512]{1,0:T(8,128)(2,1)}, u32[]{:S(2)}) copy-start(bf16[384,512]{1,0:T(8,128)(2,1)} %param.7) | copy-start | bytes 1179652
  7.2 12.7 %copy-start.2 = (bf16[4,4,6,16,128]{4,3,2,1,0:T(8,128)(2,1)S(1)}, bf16[4,4,6,16,128]{4,3,2,1,0:T(8,128)(2,1)}, u32[]{:S(2)}) copy-start(bf16[4,4,6,16,128]{4,3,2,1,0:T(8,128)(2,1)} %param.4) | copy-start | bytes 1179652
  7.2 6.7 %copy-start.3 = (bf16[4,6,16]{2,0,1:T(4,128)(2,1)S(1)}, bf16[4,6,16]{2,0,1:T(4,128)(2,1)}, u32[]{:S(2)}) copy-start(bf16[4,6,16]{2,0,1:T(4,128)(2,1)} %param.5) | copy-start | bytes 2308
  7.2 12.7 %copy-start.4 = (f32[4,4]{1,0:T(4,128)S(1)}, f32[4,4]{1,0:T(4,128)}, u32[]{:S(2)}) copy-start(f32[4,4]{1,0:T(4,128)} %param.6) | copy-start | bytes 196
  7.2 85.6 %reduce-scatter.2.cloned.1.call-start = ((), (), s32[]{:S(2)}) async-start(), calls=%async_computation.2 | async-start | bytes 1310720 | tf_op jit(solution)/shard_map/reduce_scatter | solution.py:50
  8.6 7.7 %collective-permute-start = (f32[1,4,6,16,128]{4,1,3,2,0:T(4,128)S(1)}, f32[1,4,6,16,128]{4,1,3,2,0:T(4,128)S(1)}, u32[]{:S(2)}, u32[]{:S(2)}) collective-permute-start(f32[1,4,6,16,128]{4,1,3,2,0:T(4,128)S(1)} %get-tuple-element.10), channel_id=1, source_target_pairs={{4,0},{8,4},{12,8},{16,12},{20,16},{24,20},{28,24},{5,1},{9,5},{13... | collective-permute-start | bytes 589832 | tf_op jit(solution)/shard_map/ppermute | solution.py:18
  11.6 8.3 %collective-permute-start.1 = (f32[1,4,6,16,128]{4,1,3,2,0:T(4,128)S(1)}, f32[1,4,6,16,128]{4,1,3,2,0:T(4,128)S(1)}, u32[]{:S(2)}, u32[]{:S(2)}) collective-permute-start(f32[1,4,6,16,128]{4,1,3,2,0:T(4,128)S(1)} %get-tuple-element.11), channel_id=1, source_target_pairs={{0,4},{4,8},{8,12},{12,16},{16,20},{20,24},{24,28},{1,5},{5,9},{9,... | collective-permute-start | bytes 589832 | tf_op jit(solution)/shard_map/ppermute | solution.py:15
  22.2 9.3 %collective-permute-start.2 = (f32[1,4,6,16,128]{4,1,3,2,0:T(4,128)S(1)}, f32[1,4,6,16,128]{4,1,3,2,0:T(4,128)S(1)}, u32[]{:S(2)}, u32[]{:S(2)}) collective-permute-start(f32[1,4,6,16,128]{4,1,3,2,0:T(4,128)S(1)} %get-tuple-element.8), channel_id=1, source_target_pairs={{4,0},{8,4},{12,8},{16,12},{20,16},{24,20},{28,24},{5,1},{9,5},{13... | collective-permute-start | bytes 589832 | tf_op jit(solution)/shard_map/ppermute | solution.py:18
  27.7 8.4 %collective-permute-start.3 = (f32[1,4,6,16,128]{4,1,3,2,0:T(4,128)S(1)}, f32[1,4,6,16,128]{4,1,3,2,0:T(4,128)S(1)}, u32[]{:S(2)}, u32[]{:S(2)}) collective-permute-start(f32[1,4,6,16,128]{4,1,3,2,0:T(4,128)S(1)} %get-tuple-element.9), channel_id=1, source_target_pairs={{0,4},{4,8},{8,12},{12,16},{16,20},{20,24},{24,28},{1,5},{5,9},{9,... | collective-permute-start | bytes 589832 | tf_op jit(solution)/shard_map/ppermute | solution.py:15
  39.0 9.2 %collective-permute-start.4 = (f32[1,4,6,16,128]{4,1,3,2,0:T(4,128)S(1)}, f32[1,4,6,16,128]{4,1,3,2,0:T(4,128)S(1)}, u32[]{:S(2)}, u32[]{:S(2)}) collective-permute-start(f32[1,4,6,16,128]{4,1,3,2,0:T(4,128)S(1)} %get-tuple-element.6), channel_id=1, source_target_pairs={{4,0},{8,4},{12,8},{16,12},{20,16},{24,20},{28,24},{5,1},{9,5},{13... | collective-permute-start | bytes 589832 | tf_op jit(solution)/shard_map/ppermute | solution.py:18
  44.4 8.5 %collective-permute-start.5 = (f32[1,4,6,16,128]{4,1,3,2,0:T(4,128)S(1)}, f32[1,4,6,16,128]{4,1,3,2,0:T(4,128)S(1)}, u32[]{:S(2)}, u32[]{:S(2)}) collective-permute-start(f32[1,4,6,16,128]{4,1,3,2,0:T(4,128)S(1)} %get-tuple-element.7), channel_id=1, source_target_pairs={{0,4},{4,8},{8,12},{12,16},{16,20},{20,24},{24,28},{1,5},{5,9},{9,... | collective-permute-start | bytes 589832 | tf_op jit(solution)/shard_map/ppermute | solution.py:15
  67.5 97.8 %all-reduce.5.cloned.1.call-start = ((), (), s32[]{:S(2)}) async-start(), calls=%async_computation.3 | async-start | bytes 524288 | tf_op jit(solution)/shard_map/psum | solution.py:51
  166.2 10.2 %copy-start.1 = (f32[128,512]{0,1:T(8,128)S(1)}, f32[128,512]{0,1:T(8,128)}, u32[]{:S(2)}) copy-start(f32[128,512]{0,1:T(8,128)} %all-reduce.5.cloned.1.call-done) | copy-start | bytes 786436
Sparse Core Ops, SparseCore 0:
  67.6 25.1 reduce-scatter.1
  96.5 68.6 all-reduce.4
where the time goes:
time: 187 us; the launch traced here: 184 us
  waiting for transfers between devices  117 us (63%)
  starting transfers between devices  20.1 us (11%)
  blocking collectives  19 us (10%)
  between operations  14.2 us (8%)
  matrix products  10.5 us (6%)
  other arithmetic  2.23 us (1%)
    psum x1, waiting for transfers between devices, shards(): own_rows = lax.psum(own_rows, 'nodes')  72.4 us
    reduce_scatter x1, waiting for transfers between devices, shards(): lax.psum_scatter(partial_gram, 'cols', scatter_dimension=0, tiled=True)  25.3 us
    ppermute x3, starting transfers between devices, with_halo(): lax.ppermute(lax.slice_in_dim(block, 0, width, axis=dim), axis, backward)  13.9 us
    ppermute x3, waiting for transfers between devices, with_halo(): lax.ppermute(lax.slice_in_dim(block, block.shape[dim] - width, None, axis...  13 us
    all_to_all x1, blocking collectives, shards(): lax.all_to_all(filtered, 'cols', split_axis=0, concat_axis=1, tiled=True)  9.94 us
    all_gather x1, blocking collectives, shards(): lax.all_gather(own_rows.astype(jnp.bfloat16), 'cols', axis=0, tiled=True)  9.03 us
    dot_general x3, matrix products, operate_inner(): jnp.einsum('de,xeyzc->xdyzc', coupling, middle, precision=lax.Precision.H...  7.97 us
    ppermute x3, starting transfers between devices, with_halo(): lax.ppermute(lax.slice_in_dim(block, block.shape[dim] - width, None, axis...  6.1 us
  transfers between devices with their start and end apart: 8, of which 8 were waited for; matrix products, arithmetic and copies ran while one was open for 0% of the time, Pallas kernels for 0%

commit v1 on v0

--- a/solution.py
+++ b/solution.py
@@ -1,10 +1,16 @@
+import functools
+
 import jax
 import jax.numpy as jnp
 from jax import lax
+from jax.experimental import pallas as pl
+from jax.experimental.pallas import tpu as pltpu
 from jax.sharding import PartitionSpec as P
 
 center_value = 10.0
 half_width = 7.0
+MESH = pl.DeviceIdType.MESH
+WIDTH = 3
 
 
 def with_halo(block, sides, width):
@@ -30,7 +36,7 @@
     return (6.0 + shift_part[:, None, :, :, None]) * middle - beside + coupled
 
 
-def shards(vectors, node_shift, coupling, dual_basis):
+def shards_plain(vectors, node_shift, coupling, dual_basis):
     shift_full = node_shift.astype(jnp.float32)
 
     def advance(state):
@@ -58,6 +64,407 @@
     return (own_rows, rotated)
 
 
+def remote(src, dst, send, recv, node, col):
+    return pltpu.make_async_remote_copy(
+        src_ref=src, dst_ref=dst, send_sem=send, recv_sem=recv,
+        device_id=(node, col), device_id_type=MESH,
+    )
+
+
+def kernel(
+    nodes, cols, v_ref, shift_ref, c_ref, d_ref, gram_ref, rot_ref,
+    ghost, s0, s1, s2, shc, shb, dall, filt, frow, gacc, gsend, rsbuf, gall,
+    halo_send, halo_recv, sh_send, sh_recv, d_send, d_recv, df_send, own_sem,
+    f_send, f_recv, rs_send, rs_recv, ag_send, ag_recv, fw_send, fw_recv,
+):
+    n = lax.axis_index("nodes")
+    c = lax.axis_index("cols")
+    layers, dofs, gy, gz, width = v_ref.shape
+    slab_rows = dofs * gy * gz
+    own_rows, vecs = d_ref.shape
+    piece = width // nodes
+    sib = c + 1 - 2 * lax.rem(c, 2)
+    pairs = cols // 2
+    has_lo = n > 0
+    has_hi = n < nodes - 1
+
+    def wrap(value, count):
+        return lax.rem(value + count, count)
+
+    barrier = pltpu.get_barrier_semaphore()
+    partners = []
+    for dn in range(nodes):
+        for dc in range(pairs):
+            if dn or dc:
+                partners.append((wrap(n + dn, nodes), wrap(c + 2 * dc, cols)))
+    for dc in range(pairs):
+        partners.append((n, wrap(sib + 2 * dc, cols)))
+    for partner in partners:
+        pl.semaphore_signal(barrier, inc=1, device_id=partner, device_id_type=MESH)
+
+    own_d = pltpu.make_async_copy(
+        d_ref, dall.at[pl.ds(pl.multiple_of(c * own_rows, 16), own_rows)], own_sem.at[0]
+    )
+    own_d.start()
+    shc[2:layers + 2] = jnp.zeros_like(shc[2:layers + 2])
+    for l in range(layers):
+        shc[l + 2, 0:gy, 0:gz] = shift_ref[l].astype(jnp.float32)
+    pl.semaphore_wait(barrier, len(partners))
+
+    def up_copy(k):
+        return remote(v_ref.at[layers - 1 - k], ghost.at[k], halo_send.at[k], halo_recv.at[k], n + 1, c)
+
+    def down_copy(k):
+        return remote(
+            v_ref.at[k], ghost.at[WIDTH + k], halo_send.at[WIDTH + k], halo_recv.at[WIDTH + k], n - 1, c
+        )
+
+    def up_shift():
+        return remote(shc.at[pl.ds(layers, 2)], shc.at[pl.ds(0, 2)], sh_send.at[0], sh_recv.at[0], n + 1, c)
+
+    def down_shift():
+        return remote(
+            shc.at[pl.ds(2, 2)], shc.at[pl.ds(layers + 2, 2)], sh_send.at[1], sh_recv.at[1], n - 1, c
+        )
+
+    @pl.when(has_hi)
+    def _():
+        up_copy(0).start()
+        up_shift().start()
+
+    @pl.when(has_lo)
+    def _():
+        down_copy(0).start()
+        down_shift().start()
+
+    for k in range(1, WIDTH):
+        @pl.when(has_hi)
+        def _(k=k):
+            up_copy(k).start()
+
+        @pl.when(has_lo)
+        def _(k=k):
+            down_copy(k).start()
+
+    def d_rows(q):
+        return dall.at[pl.ds(pl.multiple_of(q * own_rows, 16), own_rows)]
+
+    def d_copy(j):
+        target = sib if j == 0 else wrap(c + 2 * j, cols)
+        return remote(d_ref, d_rows(c), d_send.at[j], d_recv.at[j], n, target)
+
+    def d_forward(j):
+        source = wrap(c - 2 * j, cols)
+        return remote(d_rows(source), d_rows(source), df_send.at[j], d_recv.at[pairs + j], n, sib)
+
+    for j in list(range(1, pairs)) + [0]:
+        d_copy(j).start()
+
+    s0[:, :, 0] = jnp.zeros_like(s0[:, :, 0])
+    s0[:, :, gy + 1] = jnp.zeros_like(s0[:, :, 0])
+    s1[:, :, 0] = jnp.zeros_like(s1[:, :, 0])
+    s1[:, :, gy + 1] = jnp.zeros_like(s1[:, :, 0])
+    s2[:, :, 0] = jnp.zeros_like(s2[:, :, 0])
+    s2[:, :, gy + 1] = jnp.zeros_like(s2[:, :, 0])
+
+    @pl.when(jnp.logical_not(has_lo))
+    def _():
+        s0[0:3] = jnp.zeros_like(s0[0:3])
+        s1[0:2] = jnp.zeros_like(s1[0:2])
+        s2[0:1] = jnp.zeros_like(s2[0:1])
+
+    @pl.when(jnp.logical_not(has_hi))
+    def _():
+        s0[layers + 3:] = jnp.zeros_like(s0[0:3])
+        s1[layers + 2:] = jnp.zeros_like(s1[0:2])
+        s2[layers + 1:] = jnp.zeros_like(s2[0:1])
+
+    row_id = lax.broadcasted_iota(jnp.int32, (gz, width), 0)
+    eye = lax.broadcasted_iota(jnp.int32, (gz, gz), 0) == lax.broadcasted_iota(jnp.int32, (gz, gz), 1)
+
+    def spread(l):
+        for y in range(gy):
+            row = jnp.broadcast_to(shc[l + 2, y:y + 1, 0:gz], (gz, gz))
+            column = jnp.sum(jnp.where(eye, row, 0.0), axis=1, keepdims=True)
+            shb[l + 2, y] = jnp.broadcast_to(column + (6.0 - center_value), (gz, width))
+
+    def load(target, block):
+        s0[target, :, 1:gy + 1] = block.astype(jnp.float32)
+
+    def beside(mid):
+        down = jnp.where(row_id > 0, pltpu.roll(mid, 1, 0), 0.0)
+        up = jnp.where(row_id < gz - 1, pltpu.roll(mid, gz - 1, 0), 0.0)
+        return down + up
+
+    coef = [[c_ref[d, e] for e in range(dofs)] for d in range(dofs)]
+
+    def stencil(src, at, l, scale, y):
+        mids = [src[at, e, y + 1] for e in range(dofs)]
+        base = shb[l + 2, y]
+        out = []
+        for d in range(dofs):
+            near = src[at - 1, d, y + 1] + src[at + 1, d, y + 1]
+            near = near + (src[at, d, y] + src[at, d, y + 2]) + beside(mids[d])
+            total = (base + coef[d][d]) * mids[d] - near
+            for e in range(dofs):
+                if e != d:
+                    total = total + coef[d][e] * mids[e]
+            out.append(total * scale)
+        return out
+
+    def one(l):
+        @pl.loop(0, gy)
+        def _(y):
+            for d, value in enumerate(stencil(s0, l + 3, l, 1.0 / half_width, y)):
+                s1[l + 2, d, y + 1] = value
+
+    def two(l):
+        @pl.loop(0, gy)
+        def _(y):
+            for d, value in enumerate(stencil(s1, l + 2, l, 2.0 / half_width, y)):
+                s2[l + 1, d, y + 1] = value - s0[l + 3, d, y + 1]
+
+    def three(l):
+        @pl.loop(0, gy)
+        def _(y):
+            for d, value in enumerate(stencil(s2, l + 1, l, 2.0 / half_width, y)):
+                value = value - s1[l + 2, d, y + 1]
+                at = pl.multiple_of(l * slab_rows + (d * gy + y) * gz, 16)
+                filt[pl.ds(at, gz), :] = value.astype(filt.dtype)
+
+    inner = range(1, layers - 1)
+    ends = (0, layers - 1)
+
+    for l in range(layers):
+        load(l + 3, v_ref[l])
+        spread(l)
+    for l in inner:
+        one(l)
+
+    @pl.when(has_lo)
+    def _():
+        up_copy(0).wait_recv()
+        load(2, ghost[0])
+        up_shift().wait_recv()
+        spread(-1)
+        spread(-2)
+
+    @pl.when(has_hi)
+    def _():
+        down_copy(0).wait_recv()
+        load(layers + 3, ghost[WIDTH])
+        down_shift().wait_recv()
+        spread(layers)
+        spread(layers + 1)
+
+    for l in ends:
+        one(l)
+    for l in inner:
+        two(l)
+
+    @pl.when(has_lo)
+    def _():
+        up_copy(1).wait_recv()
+        load(1, ghost[1])
+        one(-1)
+
+    @pl.when(has_hi)
+    def _():
+        down_copy(1).wait_recv()
+        load(layers + 4, ghost[WIDTH + 1])
+        one(layers)
+
+    for l in ends:
+        two(l)
+    for l in inner:
+        three(l)
+
+    for j in range(1, pairs):
+        d_copy(j).wait_recv()
+        d_forward(j).start()
+
+    @pl.when(has_lo)
+    def _():
+        up_copy(2).wait_recv()
+        load(0, ghost[2])
+        one(-2)
+        two(-1)
+
+    @pl.when(has_hi)
+    def _():
+        down_copy(2).wait_recv()
+        load(layers + 5, ghost[WIDTH + 2])
+        one(layers + 1)
+        two(layers)
+
+    for l in ends:
+        three(l)
+
+    own_d.wait()
+    d_copy(0).wait_recv()
+    for j in range(1, pairs):
+        d_forward(j).wait_recv()
+    gacc[...] = lax.dot_general(
+        filt[...], dall[...], (((0,), (0,)), ((), ())), preferred_element_type=jnp.float32
+    )
+    gsend[...] = gacc[...].astype(gsend.dtype)
+
+    def rs_copy(j):
+        target = wrap(n + j, nodes)
+        return remote(
+            gsend.at[pl.ds(pl.multiple_of(target * piece, 16), piece)],
+            rsbuf.at[j - 1], rs_send.at[j - 1], rs_recv.at[j - 1], target, c,
+        )
+
+    for j in range(1, nodes):
+        rs_copy(j).start()
+
+    def f_copy(j):
+        target = wrap(c + j, cols)
+        return remote(
+            filt.at[pl.ds(pl.multiple_of(target * own_rows, 16), own_rows)],
+            frow.at[:, pl.ds(pl.multiple_of(c * width, 128), width)],
+            f_send.at[j - 1], f_recv.at[j - 1], n, target,
+        )
+
+    for j in range(1, cols):
+        f_copy(j).start()
+    own_f = pltpu.make_async_copy(
+        filt.at[pl.ds(pl.multiple_of(c * own_rows, 16), own_rows)],
+        frow.at[:, pl.ds(pl.multiple_of(c * width, 128), width)],
+        own_sem.at[1],
+    )
+    own_f.start()
+
+    total = gacc[pl.ds(pl.multiple_of(n * piece, 16), piece), :]
+    for j in range(1, nodes):
+        rs_copy(j).wait_recv()
+        total = total + rsbuf[j - 1].astype(jnp.float32)
+
+    def g_rows(node, col):
+        return gall.at[pl.ds(pl.multiple_of(col * width + node * piece, 16), piece)]
+
+    gall[pl.ds(pl.multiple_of(c * width + n * piece, 16), piece), :] = total.astype(gall.dtype)
+
+    def ag_copy(dn, dc):
+        slot = dn * pairs + dc
+        return remote(
+            g_rows(n, c), g_rows(n, c), ag_send.at[slot], ag_recv.at[slot],
+            wrap(n + dn, nodes), wrap(c + 2 * dc, cols),
+        )
+
+    def fw_copy(dn, dc):
+        slot = dn * pairs + dc
+        rows = g_rows(wrap(n - dn, nodes), wrap(c - 2 * dc, cols))
+        return remote(rows, rows, fw_send.at[slot], fw_recv.at[slot], n, sib)
+
+    steps = [(dn, dc) for dn in range(nodes) for dc in range(pairs)]
+    fw_copy(0, 0).start()
+    for dn, dc in steps[1:]:
+        ag_copy(dn, dc).start()
+    for dn, dc in steps[1:]:
+        ag_copy(dn, dc).wait_recv()
+        fw_copy(dn, dc).start()
+    own_f.wait()
+    for j in range(1, cols):
+        f_copy(j).wait_recv()
+    for dn, dc in steps:
+        fw_copy(dn, dc).wait_recv()
+
+    rotated = lax.dot_general(
+        frow[...], gall[...], (((1,), (1,)), ((), ())), preferred_element_type=jnp.float32
+    )
+    rot_ref[...] = (rotated * vecs ** (-0.5)).astype(rot_ref.dtype)
+    unit = (
+        lax.broadcasted_iota(jnp.int32, (width, width), 0)
+        == lax.broadcasted_iota(jnp.int32, (width, width), 1)
+    ).astype(jnp.float32).astype(gall.dtype)
+    gram_ref[...] = lax.dot_general(
+        unit, gall[:, pl.ds(pl.multiple_of(c * width, 128), width)],
+        (((1,), (1,)), ((), ())), preferred_element_type=jnp.float32,
+    )
+
+    @pl.when(has_hi)
+    def _():
+        for k in range(WIDTH):
+            up_copy(k).wait_send()
+        up_shift().wait_send()
+
+    @pl.when(has_lo)
+    def _():
+        for k in range(WIDTH):
+            down_copy(k).wait_send()
+        down_shift().wait_send()
+
+    for j in range(pairs):
+        d_copy(j).wait_send()
+    for j in range(1, pairs):
+        d_forward(j).wait_send()
+    for j in range(1, cols):
+        f_copy(j).wait_send()
+    for j in range(1, nodes):
+        rs_copy(j).wait_send()
+    for dn, dc in steps[1:]:
+        ag_copy(dn, dc).wait_send()
+    for dn, dc in steps:
+        fw_copy(dn, dc).wait_send()
+
+
+def shards_fused(nodes, cols, vectors, node_shift, coupling, dual_basis):
+    layers, dofs, gy, gz, width = vectors.shape
+    own_rows, vecs = dual_basis.shape
+    slab = layers * dofs * gy * gz
+    piece = width // nodes
+    pairs = cols // 2
+    f32, bf16 = jnp.float32, jnp.bfloat16
+    dma = pltpu.SemaphoreType.DMA
+    vmem = pl.BlockSpec(memory_space=pltpu.VMEM)
+    return pl.pallas_call(
+        functools.partial(kernel, nodes, cols),
+        out_shape=(
+            jax.ShapeDtypeStruct((vecs // cols, vecs), f32),
+            jax.ShapeDtypeStruct((own_rows, vecs), bf16),
+        ),
+        in_specs=[vmem, vmem, pl.BlockSpec(memory_space=pltpu.SMEM), vmem],
+        out_specs=(vmem, vmem),
+        scratch_shapes=[
+            pltpu.VMEM((2 * WIDTH, dofs, gy, gz, width), bf16),
+            pltpu.VMEM((layers + 6, dofs, gy + 2, gz, width), f32),
+            pltpu.VMEM((layers + 4, dofs, gy + 2, gz, width), f32),
+            pltpu.VMEM((layers + 2, dofs, gy + 2, gz, width), f32),
+            pltpu.VMEM((layers + 4, 8, 128), f32),
+            pltpu.VMEM((layers + 4, gy, gz, width), f32),
+            pltpu.VMEM((slab, vecs), bf16),
+            pltpu.VMEM((slab, width), bf16),
+            pltpu.VMEM((own_rows, vecs), bf16),
+            pltpu.VMEM((width, vecs), f32),
+            pltpu.VMEM((width, vecs), bf16),
+            pltpu.VMEM((nodes - 1, piece, vecs), bf16),
+            pltpu.VMEM((vecs, vecs), bf16),
+            dma((2 * WIDTH,)), dma((2 * WIDTH,)), dma((2,)), dma((2,)),
+            dma((pairs,)), dma((2 * pairs,)), dma((pairs,)), dma((2,)),
+            dma((cols - 1,)), dma((cols - 1,)), dma((nodes - 1,)), dma((nodes - 1,)),
+            dma((nodes * pairs,)), dma((nodes * pairs,)), dma((nodes * pairs,)), dma((nodes * pairs,)),
+        ],
+        compiler_params=pltpu.CompilerParams(
+            collective_id=0, has_side_effects=True, vmem_limit_bytes=40 * 1024 * 1024
+        ),
+        cost_estimate=pl.CostEstimate(flops=4 * own_rows * vecs * vecs, bytes_accessed=4 << 20, transcendentals=0),
+    )(vectors, node_shift, coupling, dual_basis)
+
+
+def shards(nodes, cols, vectors, node_shift, coupling, dual_basis):
+    layers, dofs, gy, gz, width = vectors.shape
+    own_rows = dual_basis.shape[0]
+    fits = (
+        width % (16 * nodes) == 0 and width % 128 == 0 and gz == 16 and gy <= 8 and layers >= WIDTH
+        and cols % 2 == 0 and own_rows % 16 == 0 and own_rows * cols == layers * dofs * gy * gz
+    )
+    if fits:
+        return shards_fused(nodes, cols, vectors, node_shift, coupling, dual_basis)
+    return shards_plain(vectors, node_shift, coupling, dual_basis)
+
+
 def solution(mesh):
     placed = (
         P("nodes", None, None, None, "cols"),
@@ -66,7 +473,7 @@
         P(("nodes", "cols"), None),
     )
     return jax.shard_map(
-        shards,
+        functools.partial(shards, mesh.shape["nodes"], mesh.shape["cols"]),
         mesh=mesh,
         in_specs=placed,
         out_specs=(P("cols", None), P(("nodes", "cols"), None)),

time: 187 us -> 40.7 us (0.22); the launches traced: 184 us -> 40.4 us
  waiting for transfers between devices: 117 us -> 0 us
  Pallas kernels: 0 us -> 35.6 us
  starting transfers between devices: 20.1 us -> 0 us
  blocking collectives: 19 us -> 0 us
  between operations: 14.2 us -> 0.65 us
  matrix products: 10.5 us -> 0 us
  local copies, waits for them, and re-layouts: 1.23 us -> 4.15 us
  other arithmetic: 2.23 us -> 0 us
    psum x1 -> x0, waiting for transfers between devices: 72.4 us -> none  [shards(): own_rows = lax.psum(own_rows, 'nodes')]
    pallas_call x0 -> x1, Pallas kernels: none -> 35.6 us  [shards_fused(): pl.pallas_call(functools.partial(kernel, nodes, cols), out_shape=(jax.Sha...]
    reduce_scatter x1 -> x0, waiting for transfers between devices: 25.3 us -> none  [shards(): lax.psum_scatter(partial_gram, 'cols', scatter_dimension=0, tiled=True)]
    ppermute x6 -> x0, starting transfers between devices: 20 us -> none  [the longest x3 13.9 us: with_halo(): lax.ppermute(lax.slice_in_dim(block, 0, width, axis=dim), axis, backward)]
    ppermute x6 -> x0, waiting for transfers between devices: 19.1 us -> none  [the longest x3 13 us: with_halo(): lax.ppermute(lax.slice_in_dim(block, block.shape[dim] - width, None, axis...]
    dot_general x5 -> x0, matrix products: 10.5 us -> none  [the longest x3 7.97 us: operate_inner(): jnp.einsum('de,xeyzc->xdyzc', coupling, middle, precision=lax.Precision.H...]
    all_to_all x1 -> x0, blocking collectives: 9.94 us -> none  [shards(): lax.all_to_all(filtered, 'cols', split_axis=0, concat_axis=1, tiled=True)]
    all_gather x1 -> x0, blocking collectives: 9.03 us -> none  [shards(): lax.all_gather(own_rows.astype(jnp.bfloat16), 'cols', axis=0, tiled=True)]
  transfers between devices with their start and end apart: 8 -> 0, of which waited for: 8 -> 0; matrix products, arithmetic and copies ran while one was open for 0% -> 0% of each run, Pallas kernels for 0% -> 0%
where the time goes in v1:
time: 40.7 us; the launch traced here: 40.4 us
  Pallas kernels  35.6 us (87%)
  local copies, waits for them, and re-layouts  4.15 us (10%)
  between operations  0.65 us (2%)
    pallas_call x1, Pallas kernels, shards_fused(): pl.pallas_call(functools.partial(kernel, nodes, cols), out_shape=(jax.Sha...  35.6 us
    unnamed x9, local copies, waits for them, and re-layouts  4.15 us

profile of v1, /device:TPU:27, one launch (start us, length us, event | category | flops | bytes accessed | tf_op | source)
XLA Modules:
  0.0 40.4 jit_solution(16949619835682997756)
XLA Ops:
  0.6 0.0 copy-start.2
  0.6 0.7 %copy.6.shift_ref = bf16[4,6,16]{2,1,0:T(8,128)(2,1)S(1)} copy(bf16[4,6,16]{2,0,1:T(4,128)(2,1)} %param.5) | data formatting | bytes 1536 | tf_op args[1]
  1.3 0.0 copy-done.2
  1.3 0.0 copy-start
  1.3 1.0 %copy-done = bf16[4,4,6,16,128]{4,3,2,1,0:T(8,128)(2,1)S(1)} copy-done((bf16[4,4,6,16,128]{4,3,2,1,0:T(8,128)(2,1)S(1)}, bf16[4,4,6,16,128]{4,3,2,1,0:T(8,128)(2,1)}, u32[]{:S(2)}) %copy-start) | copy-done | bytes 393240
  2.3 0.0 copy-start.1
  2.3 1.0 %copy-done.1 = bf16[384,512]{1,0:T(8,128)(2,1)S(1)} copy-done((bf16[384,512]{1,0:T(8,128)(2,1)S(1)}, bf16[384,512]{1,0:T(8,128)(2,1)}, u32[]{:S(2)}) %copy-start.1) | copy-done | bytes 393240
  3.3 35.6 %shard_map.59 = (f32[128,512]{1,0:T(8,128)S(1)}, bf16[384,512]{1,0:T(8,128)(2,1)S(1)}) custom-call(bf16[4,4,6,16,128]{4,3,2,1,0:T(8,128)(2,1)S(1)} %copy-done, bf16[4,6,16]{2,1,0:T(8,128)(2,1)S(1)} %copy.6.shift_ref, f32[4,4]{1,0:T(4,128)S(1)} %copy-done.2, bf16[384,512]{1,0:T(8,128)(2,1)S(1)} %copy-done.1), custom_call_target="tpu_custom_call" | custom-call | flops 402653184 | bytes 4194304 | tf_op jit(solution)/shard_map/pallas_call | solution.py:422
  39.0 0.7 %copy.9 = f32[128,512]{1,0:T(8,128)} copy(f32[128,512]{1,0:T(8,128)S(1)} %get-tuple-element.4) | data formatting | bytes 524288
  39.7 0.7 %copy.10 = bf16[384,512]{1,0:T(8,128)(2,1)} copy(bf16[384,512]{1,0:T(8,128)(2,1)S(1)} %get-tuple-element.5) | data formatting | bytes 786432
Async XLA Ops:
  0.6 0.7 %copy-start.2 = (f32[4,4]{1,0:T(4,128)S(1)}, f32[4,4]{1,0:T(4,128)}, u32[]{:S(2)}) copy-start(f32[4,4]{1,0:T(4,128)} %c_ref.1) | copy-start | bytes 196
  1.3 1.0 %copy-start = (bf16[4,4,6,16,128]{4,3,2,1,0:T(8,128)(2,1)S(1)}, bf16[4,4,6,16,128]{4,3,2,1,0:T(8,128)(2,1)}, u32[]{:S(2)}) copy-start(bf16[4,4,6,16,128]{4,3,2,1,0:T(8,128)(2,1)} %v_ref.1) | copy-start | bytes 1179652
  2.3 1.0 %copy-start.1 = (bf16[384,512]{1,0:T(8,128)(2,1)S(1)}, bf16[384,512]{1,0:T(8,128)(2,1)}, u32[]{:S(2)}) copy-start(bf16[384,512]{1,0:T(8,128)(2,1)} %d_ref.1) | copy-start | bytes 1179652

commit v2 on v1

--- a/solution.py
+++ b/solution.py
@@ -72,8 +72,8 @@
 
 
 def kernel(
-    nodes, cols, v_ref, shift_ref, c_ref, d_ref, gram_ref, rot_ref,
-    ghost, s0, s1, s2, shc, shb, dall, filt, frow, gacc, gsend, rsbuf, gall,
+    nodes, cols, v_hbm, shift_ref, c_ref, d_hbm, frow, gall,
+    v_ref, ghost, s0, s1, s2, shc, shb, dall, filt, gacc, gsend, rsbuf,
     halo_send, halo_recv, sh_send, sh_recv, d_send, d_recv, df_send, own_sem,
     f_send, f_recv, rs_send, rs_recv, ag_send, ag_recv, fw_send, fw_recv,
 ):
@@ -81,7 +81,7 @@
     c = lax.axis_index("cols")
     layers, dofs, gy, gz, width = v_ref.shape
     slab_rows = dofs * gy * gz
-    own_rows, vecs = d_ref.shape
+    own_rows, vecs = d_hbm.shape
     piece = width // nodes
     sib = c + 1 - 2 * lax.rem(c, 2)
     pairs = cols // 2
@@ -102,64 +102,15 @@
     for partner in partners:
         pl.semaphore_signal(barrier, inc=1, device_id=partner, device_id_type=MESH)
 
+    own_v = pltpu.make_async_copy(v_hbm, v_ref, own_sem.at[2])
+    own_v.start()
     own_d = pltpu.make_async_copy(
-        d_ref, dall.at[pl.ds(pl.multiple_of(c * own_rows, 16), own_rows)], own_sem.at[0]
+        d_hbm, dall.at[pl.ds(pl.multiple_of(c * own_rows, 16), own_rows)], own_sem.at[0]
     )
     own_d.start()
     shc[2:layers + 2] = jnp.zeros_like(shc[2:layers + 2])
     for l in range(layers):
-        shc[l + 2, 0:gy, 0:gz] = shift_ref[l].astype(jnp.float32)
-    pl.semaphore_wait(barrier, len(partners))
-
-    def up_copy(k):
-        return remote(v_ref.at[layers - 1 - k], ghost.at[k], halo_send.at[k], halo_recv.at[k], n + 1, c)
-
-    def down_copy(k):
-        return remote(
-            v_ref.at[k], ghost.at[WIDTH + k], halo_send.at[WIDTH + k], halo_recv.at[WIDTH + k], n - 1, c
-        )
-
-    def up_shift():
-        return remote(shc.at[pl.ds(layers, 2)], shc.at[pl.ds(0, 2)], sh_send.at[0], sh_recv.at[0], n + 1, c)
-
-    def down_shift():
-        return remote(
-            shc.at[pl.ds(2, 2)], shc.at[pl.ds(layers + 2, 2)], sh_send.at[1], sh_recv.at[1], n - 1, c
-        )
-
-    @pl.when(has_hi)
-    def _():
-        up_copy(0).start()
-        up_shift().start()
-
-    @pl.when(has_lo)
-    def _():
-        down_copy(0).start()
-        down_shift().start()
-
-    for k in range(1, WIDTH):
-        @pl.when(has_hi)
-        def _(k=k):
-            up_copy(k).start()
-
-        @pl.when(has_lo)
-        def _(k=k):
-            down_copy(k).start()
-
-    def d_rows(q):
-        return dall.at[pl.ds(pl.multiple_of(q * own_rows, 16), own_rows)]
-
-    def d_copy(j):
-        target = sib if j == 0 else wrap(c + 2 * j, cols)
-        return remote(d_ref, d_rows(c), d_send.at[j], d_recv.at[j], n, target)
-
-    def d_forward(j):
-        source = wrap(c - 2 * j, cols)
-        return remote(d_rows(source), d_rows(source), df_send.at[j], d_recv.at[pairs + j], n, sib)
-
-    for j in list(range(1, pairs)) + [0]:
-        d_copy(j).start()
-
+        shc[l + 2, 0:gy, 0:gz] = shift_ref[:, l].astype(jnp.float32)
     s0[:, :, 0] = jnp.zeros_like(s0[:, :, 0])
     s0[:, :, gy + 1] = jnp.zeros_like(s0[:, :, 0])
     s1[:, :, 0] = jnp.zeros_like(s1[:, :, 0])
@@ -235,11 +186,63 @@
     inner = range(1, layers - 1)
     ends = (0, layers - 1)
 
+    own_v.wait()
     for l in range(layers):
         load(l + 3, v_ref[l])
         spread(l)
+    own_d.wait()
     for l in inner:
         one(l)
+    pl.semaphore_wait(barrier, len(partners))
+
+    def up_copy(k):
+        return remote(v_ref.at[layers - 1 - k], ghost.at[k], halo_send.at[k], halo_recv.at[k], n + 1, c)
+
+    def down_copy(k):
+        return remote(
+            v_ref.at[k], ghost.at[WIDTH + k], halo_send.at[WIDTH + k], halo_recv.at[WIDTH + k], n - 1, c
+        )
+
+    def up_shift():
+        return remote(shc.at[pl.ds(layers, 2)], shc.at[pl.ds(0, 2)], sh_send.at[0], sh_recv.at[0], n + 1, c)
+
+    def down_shift():
+        return remote(
+            shc.at[pl.ds(2, 2)], shc.at[pl.ds(layers + 2, 2)], sh_send.at[1], sh_recv.at[1], n - 1, c
+        )
+
+    @pl.when(has_hi)
+    def _():
+        up_copy(0).start()
+        up_shift().start()
+
+    @pl.when(has_lo)
+    def _():
+        down_copy(0).start()
+        down_shift().start()
+
+    for k in range(1, WIDTH):
+        @pl.when(has_hi)
+        def _(k=k):
+            up_copy(k).start()
+
+        @pl.when(has_lo)
+        def _(k=k):
+            down_copy(k).start()
+
+    def d_rows(q):
+        return dall.at[pl.ds(pl.multiple_of(q * own_rows, 16), own_rows)]
+
+    def d_copy(j):
+        target = sib if j == 0 else wrap(c + 2 * j, cols)
+        return remote(d_rows(c), d_rows(c), d_send.at[j], d_recv.at[j], n, target)
+
+    def d_forward(j):
+        source = wrap(c - 2 * j, cols)
+        return remote(d_rows(source), d_rows(source), df_send.at[j], d_recv.at[pairs + j], n, sib)
+
+    for j in list(range(1, pairs)) + [0]:
+        d_copy(j).start()
 
     @pl.when(has_lo)
     def _():
@@ -300,7 +303,6 @@
     for l in ends:
         three(l)
 
-    own_d.wait()
     d_copy(0).wait_recv()
     for j in range(1, pairs):
         d_forward(j).wait_recv()
@@ -371,19 +373,6 @@
     for dn, dc in steps:
         fw_copy(dn, dc).wait_recv()
 
-    rotated = lax.dot_general(
-        frow[...], gall[...], (((1,), (1,)), ((), ())), preferred_element_type=jnp.float32
-    )
-    rot_ref[...] = (rotated * vecs ** (-0.5)).astype(rot_ref.dtype)
-    unit = (
-        lax.broadcasted_iota(jnp.int32, (width, width), 0)
-        == lax.broadcasted_iota(jnp.int32, (width, width), 1)
-    ).astype(jnp.float32).astype(gall.dtype)
-    gram_ref[...] = lax.dot_general(
-        unit, gall[:, pl.ds(pl.multiple_of(c * width, 128), width)],
-        (((1,), (1,)), ((), ())), preferred_element_type=jnp.float32,
-    )
-
     @pl.when(has_hi)
     def _():
         for k in range(WIDTH):
@@ -410,6 +399,24 @@
         fw_copy(dn, dc).wait_send()
 
 
+def finish(cols, frow, gall, gram_ref, rot_ref):
+    vecs = gall.shape[0]
+    width = vecs // cols
+    c = lax.axis_index("cols")
+    rotated = lax.dot_general(
+        frow[...], gall[...], (((1,), (1,)), ((), ())), preferred_element_type=jnp.float32
+    )
+    rot_ref[...] = (rotated * vecs ** (-0.5)).astype(rot_ref.dtype)
+    unit = (
+        lax.broadcasted_iota(jnp.int32, (width, width), 0)
+        == lax.broadcasted_iota(jnp.int32, (width, width), 1)
+    ).astype(jnp.float32).astype(gall.dtype)
+    gram_ref[...] = lax.dot_general(
+        unit, gall[:, pl.ds(pl.multiple_of(c * width, 128), width)],
+        (((1,), (1,)), ((), ())), preferred_element_type=jnp.float32,
+    )
+
+
 def shards_fused(nodes, cols, vectors, node_shift, coupling, dual_basis):
     layers, dofs, gy, gz, width = vectors.shape
     own_rows, vecs = dual_basis.shape
@@ -419,15 +426,17 @@
     f32, bf16 = jnp.float32, jnp.bfloat16
     dma = pltpu.SemaphoreType.DMA
     vmem = pl.BlockSpec(memory_space=pltpu.VMEM)
-    return pl.pallas_call(
+    hbm = pl.BlockSpec(memory_space=pltpu.HBM)
+    frow, gall = pl.pallas_call(
         functools.partial(kernel, nodes, cols),
         out_shape=(
-            jax.ShapeDtypeStruct((vecs // cols, vecs), f32),
             jax.ShapeDtypeStruct((own_rows, vecs), bf16),
+            jax.ShapeDtypeStruct((vecs, vecs), bf16),
         ),
-        in_specs=[vmem, vmem, pl.BlockSpec(memory_space=pltpu.SMEM), vmem],
+        in_specs=[hbm, vmem, pl.BlockSpec(memory_space=pltpu.SMEM), hbm],
         out_specs=(vmem, vmem),
         scratch_shapes=[
+            pltpu.VMEM((layers, dofs, gy, gz, width), bf16),
             pltpu.VMEM((2 * WIDTH, dofs, gy, gz, width), bf16),
             pltpu.VMEM((layers + 6, dofs, gy + 2, gz, width), f32),
             pltpu.VMEM((layers + 4, dofs, gy + 2, gz, width), f32),
@@ -436,21 +445,30 @@
             pltpu.VMEM((layers + 4, gy, gz, width), f32),
             pltpu.VMEM((slab, vecs), bf16),
             pltpu.VMEM((slab, width), bf16),
-            pltpu.VMEM((own_rows, vecs), bf16),
             pltpu.VMEM((width, vecs), f32),
             pltpu.VMEM((width, vecs), bf16),
             pltpu.VMEM((nodes - 1, piece, vecs), bf16),
-            pltpu.VMEM((vecs, vecs), bf16),
             dma((2 * WIDTH,)), dma((2 * WIDTH,)), dma((2,)), dma((2,)),
-            dma((pairs,)), dma((2 * pairs,)), dma((pairs,)), dma((2,)),
+            dma((pairs,)), dma((2 * pairs,)), dma((pairs,)), dma((3,)),
             dma((cols - 1,)), dma((cols - 1,)), dma((nodes - 1,)), dma((nodes - 1,)),
             dma((nodes * pairs,)), dma((nodes * pairs,)), dma((nodes * pairs,)), dma((nodes * pairs,)),
         ],
         compiler_params=pltpu.CompilerParams(
-            collective_id=0, has_side_effects=True, vmem_limit_bytes=40 * 1024 * 1024
+            collective_id=0, has_side_effects=True, vmem_limit_bytes=60 * 1024 * 1024
         ),
         cost_estimate=pl.CostEstimate(flops=4 * own_rows * vecs * vecs, bytes_accessed=4 << 20, transcendentals=0),
-    )(vectors, node_shift, coupling, dual_basis)
+    )(vectors, jnp.swapaxes(node_shift, 0, 1), coupling, dual_basis)
+    return pl.pallas_call(
+        functools.partial(finish, cols),
+        out_shape=(
+            jax.ShapeDtypeStruct((vecs // cols, vecs), f32),
+            jax.ShapeDtypeStruct((own_rows, vecs), bf16),
+        ),
+        in_specs=[vmem, vmem],
+        out_specs=(vmem, vmem),
+        compiler_params=pltpu.CompilerParams(vmem_limit_bytes=60 * 1024 * 1024),
+        cost_estimate=pl.CostEstimate(flops=2 * own_rows * vecs * vecs, bytes_accessed=2 << 20, transcendentals=0),
+    )(frow, gall)
 
 
 def shards(nodes, cols, vectors, node_shift, coupling, dual_basis):

time: 40.7 us -> 39.7 us (0.975)
  local copies, waits for them, and re-layouts: 4.15 us -> 0 us
  Pallas kernels: 35.6 us -> 38.8 us
    unnamed x9 -> x0, local copies, waits for them, and re-layouts: 4.15 us -> none
    pallas_call x0 -> x1, Pallas kernels: none -> 2.4 us  [shards_fused(): pl.pallas_call(functools.partial(finish, cols), out_shape=(jax.ShapeDtype...]
    pallas_call x1, Pallas kernels: 35.6 us -> 36.4 us  [shards_fused(): pl.pallas_call(functools.partial(kernel, nodes, cols), out_shape=(jax.Sha...]
where the time goes in v2:
time: 39.7 us; the launch traced here: 39.5 us
  Pallas kernels  38.8 us (98%)
  between operations  0.64 us (2%)
    pallas_call x1, Pallas kernels, shards_fused(): pl.pallas_call(functools.partial(kernel, nodes, cols), out_shape=(jax.Sha...  36.4 us
    pallas_call x1, Pallas kernels, shards_fused(): pl.pallas_call(functools.partial(finish, cols), out_shape=(jax.ShapeDtype...  2.4 us

profile of v2, /device:TPU:27, one launch (start us, length us, event | category | flops | bytes accessed | tf_op | source)
XLA Modules:
  0.0 39.5 jit_solution(3906492884834471783)
XLA Ops:
  0.6 36.4 %shard_map.59 = (bf16[384,512]{1,0:T(8,128)(2,1)}, bf16[512,512]{1,0:T(8,128)(2,1)}) custom-call(bf16[4,4,6,16,128]{4,3,2,1,0:T(8,128)(2,1)} %v_hbm.1, bf16[6,4,16]{2,1,0:T(4,128)(2,1)} %bitcast.1, f32[4,4]{1,0:T(4,128)} %c_ref.1, bf16[384,512]{1,0:T(8,128)(2,1)} %d_hbm.1), custom_call_target="tpu_custom_call" | custom-call | flops 402653184 | bytes 4194304 | tf_op jit(solution)/shard_map/pallas_call | solution.py:430
  37.1 2.4 %shard_map.60 = (f32[128,512]{1,0:T(8,128)}, bf16[384,512]{1,0:T(8,128)(2,1)}) custom-call(bf16[384,512]{1,0:T(8,128)(2,1)} %get-tuple-element.4.frow, bf16[512,512]{1,0:T(8,128)(2,1)} %get-tuple-element.5.gall), custom_call_target="tpu_custom_call" | custom-call | flops 201326592 | bytes 2097152 | tf_op jit(solution)/shard_map/pallas_call | solution.py:461

commit v3 on v2

--- a/solution.py
+++ b/solution.py
@@ -303,24 +303,6 @@
     for l in ends:
         three(l)
 
-    d_copy(0).wait_recv()
-    for j in range(1, pairs):
-        d_forward(j).wait_recv()
-    gacc[...] = lax.dot_general(
-        filt[...], dall[...], (((0,), (0,)), ((), ())), preferred_element_type=jnp.float32
-    )
-    gsend[...] = gacc[...].astype(gsend.dtype)
-
-    def rs_copy(j):
-        target = wrap(n + j, nodes)
-        return remote(
-            gsend.at[pl.ds(pl.multiple_of(target * piece, 16), piece)],
-            rsbuf.at[j - 1], rs_send.at[j - 1], rs_recv.at[j - 1], target, c,
-        )
-
-    for j in range(1, nodes):
-        rs_copy(j).start()
-
     def f_copy(j):
         target = wrap(c + j, cols)
         return remote(
@@ -337,6 +319,24 @@
         own_sem.at[1],
     )
     own_f.start()
+
+    d_copy(0).wait_recv()
+    for j in range(1, pairs):
+        d_forward(j).wait_recv()
+    gacc[...] = lax.dot_general(
+        filt[...], dall[...], (((0,), (0,)), ((), ())), preferred_element_type=jnp.float32
+    )
+    gsend[...] = gacc[...].astype(gsend.dtype)
+
+    def rs_copy(j):
+        target = wrap(n + j, nodes)
+        return remote(
+            gsend.at[pl.ds(pl.multiple_of(target * piece, 16), piece)],
+            rsbuf.at[j - 1], rs_send.at[j - 1], rs_recv.at[j - 1], target, c,
+        )
+
+    for j in range(1, nodes):
+        rs_copy(j).start()
 
     total = gacc[pl.ds(pl.multiple_of(n * piece, 16), piece), :]
     for j in range(1, nodes):

time: 39.7 us -> 39.7 us (level)
  no operation moved by 1% of the time
where the time goes in v3:
time: 39.7 us; the launch traced here: 39.5 us
  Pallas kernels  38.8 us (98%)
  between operations  0.64 us (2%)
    pallas_call x1, Pallas kernels, shards_fused(): pl.pallas_call(functools.partial(kernel, nodes, cols), out_shape=(jax.Sha...  36.4 us
    pallas_call x1, Pallas kernels, shards_fused(): pl.pallas_call(functools.partial(finish, cols), out_shape=(jax.ShapeDtype...  2.4 us

profile of v3, /device:TPU:27, one launch (start us, length us, event | category | flops | bytes accessed | tf_op | source)
XLA Modules:
  0.0 39.5 jit_solution(16256463379073866054)
XLA Ops:
  0.6 36.4 %shard_map.59 = (bf16[384,512]{1,0:T(8,128)(2,1)}, bf16[512,512]{1,0:T(8,128)(2,1)}) custom-call(bf16[4,4,6,16,128]{4,3,2,1,0:T(8,128)(2,1)} %v_hbm.1, bf16[6,4,16]{2,1,0:T(4,128)(2,1)} %bitcast.1, f32[4,4]{1,0:T(4,128)} %c_ref.1, bf16[384,512]{1,0:T(8,128)(2,1)} %d_hbm.1), custom_call_target="tpu_custom_call" | custom-call | flops 402653184 | bytes 4194304 | tf_op jit(solution)/shard_map/pallas_call | solution.py:430
  37.0 2.4 %shard_map.60 = (f32[128,512]{1,0:T(8,128)}, bf16[384,512]{1,0:T(8,128)(2,1)}) custom-call(bf16[384,512]{1,0:T(8,128)(2,1)} %get-tuple-element.4.frow, bf16[512,512]{1,0:T(8,128)(2,1)} %get-tuple-element.5.gall), custom_call_target="tpu_custom_call" | custom-call | flops 201326592 | bytes 2097152 | tf_op jit(solution)/shard_map/pallas_call | solution.py:461
